TPU v7x, 32 devices: a whole 2x2x4 slice. The times are simulated.
32 devices in a mesh: ctx: 8 (over y, x, core), ch: 4 (over z).
Axes of the slice: x: 2, y: 2, z: 4, core: 2. Of those that a mesh axis runs over, the one named last changes fastest.
Arguments:
- gate_query: bfloat16 [2048, 8192], P('ctx', 'ch'), may hold values from -6 to 6
- gate_key: bfloat16 [2048, 8192], P('ctx', 'ch'), may hold values from -6 to 6
- value_in: bfloat16 [2048, 8192], P('ctx', 'ch'), may hold values from -6 to 6
- mr_filter: bfloat16 [128, 512], P(None, 'ch'), may hold values from -0.5 to 0.5
- pole_rates: float32 [16, 512], P(None, 'ch'), may hold values from 2.4414063e-05 to 0.05
- residues: float32 [16, 512], P(None, 'ch'), may hold values from -3 to 3
- skip_gain: float32 [8192], P('ch'), may hold values from -4 to 4
- offsets: int32 [65], replicated, may hold values from 0 to 2048, as said below
- owner_docs: int32 [32], replicated, may hold values from 0 to 63, as said below
Outputs:
- output: bfloat16 [2048, 8192], P('ctx', 'ch')
- doc_states: float32 [32, 16, 8192], P(('ctx', 'ch'))
Inputs may be any that keep to these rules, and one draw needn't show every extreme that they name: offsets[0] = 0 and offsets[64] = 2048, strictly increasing; document d holds tokens offsets[d] to offsets[d + 1] - 1. The last tokens of at most 16 documents lie among the 256 tokens of one index of ctx, and some index holds exactly 16. `owner_docs`: for some base b, slot r * 4 + k (k < 4) holds document (b + k * 8 + r) mod 64.
All inputs are finite; a program needn't handle non-finite values.
Results may differ from a plain program's by a relative error of at most 0.0049.
Values may be sent and summed in bfloat16 or wider, within the bound.
No kernel may reach another device: no remote copies, remote signals or barrier semaphores. Data moves between devices by JAX's collectives and lax.ppermute only.
A program may use at most 320 MiB of HBM per device.

v0:
```python
import jax
import jax.numpy as jnp
from jax import lax
from jax.sharding import PartitionSpec as P

MR_LEN = 128
ENDS = 16


highest = lax.Precision.HIGHEST


def from_behind(block, axis, distance):
    devices = range(lax.axis_size(axis))
    route = [(i - distance, i) for i in devices if i - distance in devices]
    return lax.ppermute(block, axis, route)


def carried_in(x, axis, combine, identity):
    peers, place = (lax.axis_size(axis), lax.axis_index(axis))
    everything = jax.tree.map(lambda part: lax.all_gather(part, axis), x)
    start = jax.tree.map(
        lambda part, zero: jnp.broadcast_to(jnp.asarray(zero, part.dtype), part.shape), x, identity
    )

    def hop(k, before):
        reached = k < place
        new = combine(before, jax.tree.map(lambda part: part[k], everything))
        return jax.tree.map(lambda a, b: jnp.where(reached, a, b), new, before)

    return lax.fori_loop(0, peers, hop, start)


def per_device(
    gate_query, gate_key, value_in, mr_filter, pole_rates, residues, skip_gain, offsets, owner_docs
):
    length, width = value_in.shape
    pole_count, groups = pole_rates.shape
    group_size = width // groups
    blocks = length // MR_LEN
    doc_count = offsets.shape[0] - 1
    my_rank = lax.axis_index("ctx")
    device_start = my_rank * length
    device_last = device_start + length - 1
    positions = device_start + jnp.arange(length, dtype=jnp.int32)
    doc_index = jnp.sum((offsets[1:][None, :] <= positions[:, None]).astype(jnp.int32), axis=1)
    starts = jnp.max(jnp.where(offsets[None, :] <= positions[:, None], offsets[None, :], 0), axis=1)
    starts_blocked = starts.reshape(blocks, MR_LEN)
    row_ids = jnp.arange(MR_LEN, dtype=jnp.int32)
    col_ids = jnp.arange(2 * MR_LEN, dtype=jnp.int32)
    block_ids = jnp.arange(blocks, dtype=jnp.int32)
    edge_rows = from_behind(value_in[length - MR_LEN :], "ctx", 1)
    tap_lag = row_ids[:, None] + MR_LEN - col_ids[None, :]
    lag_valid = (tap_lag >= 0) & (tap_lag < MR_LEN)
    tap_table = jnp.take(mr_filter, jnp.clip(tap_lag, 0, MR_LEN - 1), axis=0)
    mr_kernel = jnp.where(lag_valid[:, :, None], tap_table, jnp.zeros_like(tap_table)).transpose(
        2, 0, 1
    )
    padded = jnp.concatenate([edge_rows, value_in], axis=0)
    earlier = padded[:length].reshape(blocks, MR_LEN, width)
    current = value_in.reshape(blocks, MR_LEN, width)
    windows = jnp.concatenate([earlier, current], axis=1)

    def mr_block(unused_carry, inputs):
        window, block_starts, block_id = inputs
        source = device_start + block_id * MR_LEN - MR_LEN + col_ids
        allowed = source[None, :] >= block_starts[:, None]
        masked = jnp.where(allowed[None], mr_kernel, jnp.zeros_like(mr_kernel))
        result = jnp.einsum(
            "gij,jgc->igc",
            masked,
            window.reshape(2 * MR_LEN, groups, group_size),
            preferred_element_type=jnp.float32,
        )
        return (unused_carry, result.reshape(MR_LEN, width))

    unused_final, mr_out = lax.scan(
        mr_block, jnp.zeros((), jnp.float32), (windows, starts_blocked, block_ids)
    )
    mixed = (gate_key.astype(jnp.float32) * mr_out.reshape(length, width)).astype(jnp.bfloat16)
    step_range = jnp.arange(MR_LEN + 1, dtype=jnp.int32).astype(jnp.float32)
    powers = jnp.exp(-pole_rates[:, :, None] * step_range[None, None, :])
    scaling = jnp.sqrt(-jnp.expm1(-2.0 * pole_rates))
    li_taps = jnp.sum((residues * scaling)[:, :, None] * powers[:, :, :MR_LEN], axis=0)
    tap_gap = row_ids[:, None] - row_ids[None, :]
    li_kernel = jnp.where(
        (tap_gap >= 0)[None], jnp.take(li_taps, jnp.clip(tap_gap, 0, MR_LEN - 1), axis=1), 0.0
    )
    carry_in = powers[:, :, 1 : MR_LEN + 1].transpose(2, 0, 1) * residues[None]
    feed_weights = scaling[:, :, None] * jnp.flip(powers[:, :, :MR_LEN], axis=2)
    block_decay = powers[:, :, MR_LEN]
    mixed_blocks = mixed.reshape(blocks, MR_LEN, width)

    def li_block(mode_state, inputs):
        block_vals, block_starts, block_id = inputs
        first_pos = device_start + block_id * MR_LEN
        values = block_vals.astype(jnp.float32).reshape(MR_LEN, groups, group_size)
        allowed = first_pos + row_ids[None, :] >= block_starts[:, None]
        inner_kernel = jnp.where(allowed[None], li_kernel, 0.0)
        local_out = jnp.einsum("gij,jgc->igc", inner_kernel, values, precision=highest)
        carried = (block_starts < first_pos).astype(jnp.float32)
        local_out = local_out + jnp.einsum(
            "ing,ngc->igc", carry_in * carried[:, None, None], mode_state, precision=highest
        )
        tail_start = block_starts[MR_LEN - 1]
        take_in = (first_pos + row_ids >= tail_start).astype(jnp.float32)
        keep_gain = (tail_start < first_pos).astype(jnp.float32)
        new_state = block_decay[:, :, None] * mode_state * keep_gain + jnp.einsum(
            "ngj,jgc->ngc", feed_weights * take_in[None, None, :], values, precision=highest
        )
        return (new_state, (local_out.reshape(MR_LEN, width), mode_state))

    start_state = jnp.zeros((pole_count, groups, group_size), jnp.float32)
    through_state, (li_out, before) = lax.scan(
        li_block, start_state, (mixed_blocks, starts_blocked, block_ids)
    )
    gate_decay = jnp.exp(-pole_rates * float(length)) * (starts[length - 1] < device_start).astype(
        jnp.float32
    )

    def compose(earlier_part, later_part):
        return (
            earlier_part[0] * later_part[0],
            later_part[0][:, :, None] * earlier_part[1] + later_part[1],
        )

    entering = carried_in(
        (gate_decay, through_state),
        "ctx",
        compose,
        (jnp.ones_like(gate_decay), jnp.zeros_like(through_state)),
    )[1]
    token_steps = jnp.arange(length, dtype=jnp.int32).astype(jnp.float32) + 1.0
    continuing = (starts < device_start).astype(jnp.float32)
    lead_weights = (
        jnp.exp(-pole_rates[None] * token_steps[:, None, None])
        * residues[None]
        * continuing[:, None, None]
    )
    correction = jnp.einsum("tng,ngc->tgc", lead_weights, entering, precision=highest).reshape(
        length, width
    )
    li_total = li_out.reshape(length, width) + correction
    output = (
        gate_query.astype(jnp.float32) * (li_total + skip_gain[None, :] * mixed.astype(jnp.float32))
    ).astype(jnp.bfloat16)
    offset_ids = jnp.arange(doc_count + 1, dtype=jnp.int32)

    def lookup(indices):
        return jnp.sum(
            jnp.where(offset_ids[None, :] == indices[:, None], offsets[None, :], 0), axis=1
        )

    candidates = doc_index[0] + jnp.arange(ENDS, dtype=jnp.int32)
    end_pos = lookup(jnp.minimum(candidates + 1, doc_count)) - 1
    doc_begin = lookup(jnp.minimum(candidates, doc_count))
    present = (candidates < doc_count) & (end_pos <= device_last)
    offset_in = jnp.clip(end_pos - device_start, 0, length - 1)
    block_pick = offset_in // MR_LEN
    inside = offset_in % MR_LEN
    block_first = device_start + block_pick * MR_LEN
    picked = (
        jnp.take(mixed_blocks, block_pick, axis=0)
        .astype(jnp.float32)
        .reshape(ENDS, MR_LEN, groups, group_size)
    )
    distance = inside[:, None] - row_ids[None, :]
    usable = (distance >= 0) & (block_first[:, None] + row_ids[None, :] >= doc_begin[:, None])
    end_weights = (
        scaling[None, :, :, None]
        * jnp.exp(
            -pole_rates[None, :, :, None]
            * jnp.where(usable, distance, 0).astype(jnp.float32)[:, None, None, :]
        )
        * usable.astype(jnp.float32)[:, None, None, :]
    )
    fresh_state = jnp.einsum("kngj,kjgc->kngc", end_weights, picked, precision=highest)
    prior_state = jnp.take(before, block_pick, axis=0)
    link_gain = (doc_begin < block_first).astype(jnp.float32)[:, None, None] * jnp.exp(
        -pole_rates[None] * (inside + 1).astype(jnp.float32)[:, None, None]
    )
    end_states = fresh_state + link_gain[..., None] * prior_state
    reach_gain = (doc_begin < device_start).astype(jnp.float32)[:, None, None] * jnp.exp(
        -pole_rates[None] * (end_pos - device_start + 1).astype(jnp.float32)[:, None, None]
    )
    end_states = end_states + reach_gain[..., None] * entering[None]
    slot_total = owner_docs.shape[0]
    matches = (owner_docs[:, None] == candidates[None, :]) & present[None, :]
    chosen = jnp.argmax(matches.astype(jnp.int32), axis=1)
    slot_found = jnp.any(matches, axis=1)
    slot_states = jnp.where(
        slot_found[:, None, None, None], jnp.take(end_states, chosen, axis=0), 0.0
    )
    slot_states = slot_states.reshape(slot_total, pole_count, width)
    summed = lax.psum_scatter(slot_states, "ctx", scatter_dimension=0, tiled=True)
    doc_states = lax.all_to_all(summed, "ch", split_axis=0, concat_axis=2, tiled=True)
    return (output, doc_states)


def solution(mesh):
    placed = (
        P("ctx", "ch"),
        P("ctx", "ch"),
        P("ctx", "ch"),
        P(None, "ch"),
        P(None, "ch"),
        P(None, "ch"),
        P("ch"),
        P(),
        P(),
    )
    return jax.shard_map(
        per_device,
        mesh=mesh,
        in_specs=placed,
        out_specs=(P("ctx", "ch"), P(("ctx", "ch"), None, None)),
        check_vma=False,
    )
```

profile of v0, /device:TPU:0, one launch (start us, length us, event | category | flops | bytes accessed | tf_op | source)
XLA Modules:
  0.0 525.4 jit_solution(7754590186397095729)
XLA Ops:
  7.2 1.9 slice.30
  9.1 3.1 collective-permute-start
  20.2 1.4 select_reduce_fusion.1
  28.6 2.0 copy.134
  30.7 2.5 fusion.57
  34.1 1.5 rev.4
  35.6 59.6 %gather_fusion.1 = f32[16384,128]{1,0:T(8,128)} fusion(f32[128,128]{0,1:T(8,128)S(1)} %copy.131, s32[16384]{0:T(1024)} %fusion.70), kind=kCustom, calls=%fused_computation.1 | custom fusion | bytes 16842752 | tf_op jit(solution)/shard_map/jit(_take)/gather | solution.py:87
  95.2 9.3 %copy.132 = f32[128,128,128]{1,0,2:T(8,128)} copy(f32[128,128,128]{2,1,0:T(8,128)} %bitcast.145) | data formatting | bytes 16777216 | tf_op jit(solution)/shard_map/jit(_take)/gather | solution.py:87
  104.5 114.1 %gather_fusion = bf16[32768,128]{1,0:T(8,128)(2,1)} fusion(bf16[128,128]{1,0:T(8,128)(2,1)S(1)} %copy-done, s32[32768]{0:T(1024)S(1)} %broadcast_clamp_fusion), kind=kCustom, calls=%fused_computation | custom fusion | bytes 16908288 | tf_op jit(solution)/shard_map/jit(_take)/gather | solution.py:55
  218.6 12.8 %copy.126 = bf16[128,256,128]{1,0,2:T(8,128)(2,1)} copy(bf16[128,256,128]{2,1,0:T(8,128)(2,1)} %bitcast.144) | data formatting | bytes 16777216 | tf_op jit(solution)/shard_map/jit(_take)/gather | solution.py:55
  232.8 7.6 %select_bitcast_fusion.1 = bf16[128,128,256]{2,1,0:T(8,128)(2,1)} fusion(bf16[128,256,128]{1,0,2:T(8,128)(2,1)} %copy.126, pred[128,256]{1,0:T(8,128)(4,1)S(1)} %copy-done.11, pred[128,256]{1,0:T(8,128)(4,1)S(1)} %get-tuple-element.525), kind=kLoop, calls=%fused_computation.60 | loop fusion | flops 8388608 | bytes 16842752 | tf_op jit(solution)/shard_map/jit(_where)/select_n | solution.py:56
  240.3 8.6 %select_bitcast_fusion = f32[128,128,128]{2,1,0:T(8,128)} fusion(f32[128,128,128]{1,0,2:T(8,128)} %copy.132, pred[128,128]{1,0:T(8,128)(4,1)S(1)} %copy-done.12, pred[128,128]{1,0:T(8,128)(4,1)S(1)} %copy-done.13), kind=kLoop, calls=%fused_computation.54 | loop fusion | flops 4194304 | bytes 16809984 | tf_op jit(solution)/shard_map/jit(_where)/select_n | solution.py:86
  250.1 1.5 pad_maximum_fusion
  251.6 1.6 broadcast.748.clone2
  253.2 25.0 %while.42 = (s32[]{:T(128)}, f32[2,128,2048]{2,1,0:T(8,128)}, bf16[2,256,2048]{2,1,0:T(8,128)(2,1)}, s32[2]{0:T(128)S(1)}, s32[]{:T(128)}, /*index=5*/s32[2,128]...) while((s32[]{:T(128)}, f32[2,128,2048]{2,1,0:T(8,128)}, ...), condition=%wide.region_2.3_spmd.clone, body=%wide.region_1.2_spmd.clone.sunk | while | flops 138445056 | bytes 18943660 | solution.py:77
  256.4 6.7 %fusion.102 = f32[128,16,128]{2,1,0:T(8,128)} fusion(bf16[256,128,16]{0,2,1:T(8,128)(2,1)S(1)} %bitcast.146, bf16[128,128,256]{2,1,0:T(8,128)(2,1)} %get-tuple-element.708, pred[128,256]{1,0:T(8,128)(4,1)S(1)} %broadcast_compare_fusion.4), kind=kOutput, calls=%fused_computation.7.clone.1 | convolution fusion | flops 138412032 | bytes 10518528 | tf_op jit(solution)/shard_map/while/body/eval_jaxpr/gij,jgc->igc/dot_general | solution.py:69
  263.0 1.6 copy.164
  268.9 6.7 %fusion.102 = f32[128,16,128]{2,1,0:T(8,128)} fusion(bf16[256,128,16]{0,2,1:T(8,128)(2,1)S(1)} %bitcast.146, bf16[128,128,256]{2,1,0:T(8,128)(2,1)} %get-tuple-element.708, pred[128,256]{1,0:T(8,128)(4,1)S(1)} %broadcast_compare_fusion.4), kind=kOutput, calls=%fused_computation.7.clone.1 | convolution fusion | flops 138412032 | bytes 10518528 | tf_op jit(solution)/shard_map/while/body/eval_jaxpr/gij,jgc->igc/dot_general | solution.py:69
  275.5 1.6 copy.164
  278.2 2.1 fusion.51
  280.3 1.6 broadcast.748.clone
  281.9 46.6 %while.43 = (s32[]{:T(128)}, f32[16,128,16]{0,2,1:T(8,128)S(1)}, f32[2,128,2048]{2,1,0:T(8,128)}, f32[2,16,128,16]{1,3,2,0:T(8,128)}, f32[16,128,1]{0,1,2:T(8,12...) while((s32[]{:T(128)}, f32[16,128,16]{0,2,1:T(8,128)S(1)}, ...), condition=%wide.region_5.6_spmd.clone, body=%wide.region_4.5_spmd.clone.sunk | while | flops 506413824 | bytes 26784536 | solution.py:114
  285.7 2.4 convolution_bitcast_fusion.3
  288.1 9.8 %fusion.110 = f32[128,128,16]{0,2,1:T(8,128)} fusion(f32[128,128,16]{0,2,1:T(8,128)S(1)} %convolution_bitcast_fusion.3, bf16[128,128,16]{0,2,1:T(8,128)(2,1)S(1)} %bitcast.141, f32[128,128,128]{2,1,0:T(8,128)} %get-tuple-element.752, pred[128,128]{1,0:T(8,128)(4,1)S(1)} %broadcast_compare_fusion.5), kind=kOutput, calls=%fused_computation.23.clone.1 | convolution fusion | flops 405012480 | bytes 11026432 | tf_op jit(solution)/shard_map/while/body/eval_jaxpr/gij,jgc->igc/dot_general | solution.py:100
  297.9 2.6 copy.166
  300.5 2.4 constant_dynamic-update-slice_fusion.5
  304.0 1.4 fusion.109
  309.0 2.4 convolution_bitcast_fusion.3
  311.4 9.8 %fusion.110 = f32[128,128,16]{0,2,1:T(8,128)} fusion(f32[128,128,16]{0,2,1:T(8,128)S(1)} %convolution_bitcast_fusion.3, bf16[128,128,16]{0,2,1:T(8,128)(2,1)S(1)} %bitcast.141, f32[128,128,128]{2,1,0:T(8,128)} %get-tuple-element.752, pred[128,128]{1,0:T(8,128)(4,1)S(1)} %broadcast_compare_fusion.5), kind=kOutput, calls=%fused_computation.23.clone.1 | convolution fusion | flops 405012480 | bytes 11026432 | tf_op jit(solution)/shard_map/while/body/eval_jaxpr/gij,jgc->igc/dot_general | solution.py:100
  321.2 2.6 copy.166
  323.7 2.4 constant_dynamic-update-slice_fusion.5
  327.2 1.4 fusion.109
  329.9 1.3 copy.145
  332.5 9.5 %all-gather = f32[128,128]{1,0:T(8,128)S(1)} all-gather(f32[16,128]{1,0:T(8,128)S(1)} %get-tuple-element.520), channel_id=2, replica_groups=mesh['ctx'=8,'ch'=4] {'ctx'}, dimensions={0}, use_global_device_ids=true | all-gather | bytes 73728 | tf_op jit(solution)/shard_map/all_gather | solution.py:21
  343.2 4.6 gather_fusion.2
  347.8 12.4 %copy.142 = bf16[16,128,2048]{1,2,0:T(8,128)(2,1)} copy(bf16[16,128,2048]{2,1,0:T(8,128)(2,1)} %gather_fusion.2) | data formatting | bytes 16777216 | tf_op jit(solution)/shard_map/jit(_take)/gather | solution.py:163
  360.2 9.4 %gather_fusion.3 = f32[16,16,128,16]{1,3,2,0:T(8,128)} fusion(f32[2,16,128,16]{1,3,2,0:T(8,128)} %get-tuple-element.272, s32[1024]{0:T(1024)S(1)} %pad_clamp_fusion.1), kind=kCustom, calls=%fused_computation.3 | custom fusion | bytes 4194368 | tf_op jit(solution)/shard_map/jit(_take)/gather | solution.py:178
  369.6 8.3 %while.44 = (s32[]{:T(128)}, f32[16,128,16]{1,2,0:T(8,128)S(1)}, s32[]{:T(128)}, f32[8,16,128]{2,1,0:T(8,128)S(1)}, f32[8,16,128,16]{2,3,1,0:T(8,128)}, /*index=5*/s32[]{:T(128)}, s32[]{:T(128)}) while((s32[]{:T(128)}, f32[16,128,16]{1,2,0:T(8,128)S(1)}, s32[]{:T(128)}, f32[8,16,128]{2,1,0:T(8,128)S(1)}, ...), condition=%wide.region_7.8_spmd.clone, body=%wide.region_6.7_spmd.clone.sunk | while | flops 131076 | bytes 417905 | solution.py:31
  378.4 24.7 %fusion.31 = f32[16,16,128,16]{1,3,2,0:T(8,128)} fusion(f32[16,16,128,16]{1,3,2,0:T(8,128)} %gather_fusion.3, f32[16,128,16]{0,2,1:T(8,128)S(1)} %copy.140, f32[16,16,128]{1,2,0:T(8,128)} %copy.146, f32[16,16,128]{1,2,0:T(8,128)} %copy.145, pred[16]{0:T(512)(128)(4,1)S(1)} %copy-done.25, f32[16,128]{1,0:T(8,128)S(1)} %fusion.78, ...), kind=kOutput, calls=%fused_computation.48 | convolution fusion | flops 824705024 | bytes 13008912 | tf_op jit(solution)/shard_map/kngj,kjgc->kngc/dot_general | solution.py:177
  403.1 18.3 %gather_fusion.4 = f32[32,16,128,16]{1,3,2,0:T(8,128)} fusion(f32[16,16,128,16]{1,3,2,0:T(8,128)} %fusion.31, s32[1024]{0:T(1024)S(1)} %pad_clamp_fusion), kind=kCustom, calls=%fused_computation.4 | custom fusion | bytes 8388736 | tf_op jit(solution)/shard_map/jit(_take)/gather | solution.py:192
  421.4 19.9 %copy.148 = f32[32,16,2048]{2,1,0:T(8,128)} copy(f32[32,16,2048]{1,2,0:T(8,128)} %bitcast.140) | data formatting | bytes 8388608 | tf_op jit(solution)/shard_map/jit(_take)/gather | solution.py:192
  441.3 5.2 select_select_fusion
  446.6 52.1 %reduce-scatter.2.cloned.1.call-done = f32[4,16,2048]{2,1,0:T(8,128)} async-done(((f32[32,16,2048]{2,1,0:T(8,128)}), f32[4,16,2048]{2,1,0:T(8,128)}) %reduce-scatter.2.cloned.1.call-update) | async-done | bytes 524304 | tf_op jit(solution)/shard_map/reduce_scatter | solution.py:195
  498.7 4.6 all-to-all-start
  503.3 3.5 fusion.52
  506.7 3.0 copy.141
  509.8 3.8 fusion.50
  513.6 4.2 all-to-all-done
  (163 shorter events, 44.7 us)
Async XLA Ops:
  7.2 97.3 %copy-start = (bf16[128,128]{1,0:T(8,128)(2,1)S(1)}, bf16[128,128]{1,0:T(8,128)(2,1)}, u32[]{:S(2)}) copy-start(bf16[128,128]{1,0:T(8,128)(2,1)} %param.18) | copy-start | bytes 98308
  7.2 362.4 %all-gather.4.cloned.1.call-start = ((), (), s32[]{:S(2)}) async-start(), calls=%async_computation.3 | async-start | bytes 1179648 | tf_op jit(solution)/shard_map/all_gather | solution.py:21
  9.1 239.9 %collective-permute-start = (bf16[128,2048]{1,0:T(8,128)(2,1)}, bf16[128,2048]{1,0:T(8,128)(2,1)}, u32[]{:S(2)}, u32[]{:S(2)}) collective-permute-start(bf16[128,2048]{1,0:T(8,128)(2,1)} %slice.30), channel_id=1, source_target_pairs={{0,4},{4,8},{8,12},{12,16},{16,20},{20,24},{24,28},{1,5},{5,9},{9,... | collective-permute-start | bytes 1572872 | tf_op jit(solution)/shard_map/ppermute | solution.py:16
  14.3 11.4 %copy-start.14 = (s32[256]{0:T(256)}, s32[256]{0:T(256)S(1)}, u32[]{:S(2)}) copy-start(s32[256]{0:T(256)S(1)} %select_reduce_fusion) | copy-start | bytes 3076
  23.3 2.4 copy-start.26
  24.7 8.5 %copy-start.6 = (f32[16,128]{0,1:T(8,128)}, f32[16,128]{0,1:T(8,128)S(1)}, u32[]{:S(2)}) copy-start(f32[16,128]{0,1:T(8,128)S(1)} %copy.133) | copy-start | bytes 24580
  25.7 1.9 copy-start.8
  218.6 12.8 %copy-start.16 = (s32[16]{0:T(128)S(1)}, s32[16]{0:T(128)}, u32[]{:S(2)}) copy-start(s32[16]{0:T(128)} %get-tuple-element.455) | copy-start | bytes 196
  218.6 12.8 %copy-start.22 = (s32[16]{0:T(128)S(1)}, s32[16]{0:T(128)}, u32[]{:S(2)}) copy-start(s32[16]{0:T(128)} %get-tuple-element.508) | copy-start | bytes 196
  218.6 12.8 %copy-start.10 = (f32[16,128]{0,1:T(8,128)S(1)}, f32[16,128]{0,1:T(8,128)}, u32[]{:S(2)}) copy-start(f32[16,128]{0,1:T(8,128)} %copy.129) | copy-start | bytes 24580
  218.6 14.1 %copy-start.11 = (pred[128,256]{1,0:T(8,128)(4,1)S(1)}, pred[128,256]{1,0:T(8,128)(4,1)}, u32[]{:S(2)}) copy-start(pred[128,256]{1,0:T(8,128)(4,1)} %get-tuple-element.526) | copy-start | bytes 98308
  232.8 7.6 %copy-start.12 = (pred[128,128]{1,0:T(8,128)(4,1)S(1)}, pred[128,128]{1,0:T(8,128)(4,1)}, u32[]{:S(2)}) copy-start(pred[128,128]{1,0:T(8,128)(4,1)} %get-tuple-element.527) | copy-start | bytes 49156
  232.8 7.6 %copy-start.13 = (pred[128,128]{1,0:T(8,128)(4,1)S(1)}, pred[128,128]{1,0:T(8,128)(4,1)}, u32[]{:S(2)}) copy-start(pred[128,128]{1,0:T(8,128)(4,1)} %get-tuple-element.528) | copy-start | bytes 49156
  240.3 8.6 %copy-start.3 = (bf16[256,2048]{1,0:T(8,128)(2,1)S(1)}, bf16[256,2048]{1,0:T(8,128)(2,1)}, u32[]{:S(2)}) copy-start(bf16[256,2048]{1,0:T(8,128)(2,1)} %param.17) | copy-start | bytes 3145732
  249.0 4.2 copy-start.15
  281.9 47.8 %copy-start.23 = (f32[16]{0:T(128)S(1)}, f32[16]{0:T(128)}, u32[]{:S(2)}) copy-start(f32[16]{0:T(128)} %add_convert_fusion) | copy-start | bytes 196
  281.9 47.9 %copy-start.24 = (f32[16]{0:T(128)S(1)}, f32[16]{0:T(128)}, u32[]{:S(2)}) copy-start(f32[16]{0:T(128)} %get-tuple-element.512) | copy-start | bytes 196
  281.9 60.1 %copy-start.27 = (s32[16]{0:T(128)S(1)}, s32[16]{0:T(128)}, u32[]{:S(2)}) copy-start(s32[16]{0:T(128)} %copy-done.26) | copy-start | bytes 196
  281.9 60.1 %copy-start.18 = (pred[16]{0:T(512)(128)(4,1)S(1)}, pred[16]{0:T(512)(128)(4,1)}, u32[]{:S(2)}) copy-start(pred[16]{0:T(512)(128)(4,1)} %get-tuple-element.523) | copy-start | bytes 52
  281.9 60.2 %copy-start.20 = (s32[32]{0:T(128)S(1)}, s32[32]{0:T(128)}, u32[]{:S(2)}) copy-start(s32[32]{0:T(128)} %param.23) | copy-start | bytes 388
  281.9 60.1 %copy-start.21 = (s32[16]{0:T(128)S(1)}, s32[16]{0:T(128)}, u32[]{:S(2)}) copy-start(s32[16]{0:T(128)} %get-tuple-element.530) | copy-start | bytes 196
  281.9 61.1 %copy-start.19 = (s32[16]{0:T(128)S(1)}, s32[16]{0:T(128)}, u32[]{:S(2)}) copy-start(s32[16]{0:T(128)} %get-tuple-element.513) | copy-start | bytes 196
  300.5 3.5 copy-start.2
  323.7 3.5 copy-start.2
  329.7 169.0 %reduce-scatter.2.cloned.1.call-start = ((), (), s32[]{:S(2)}) async-start(), calls=%async_computation.2 | async-start | bytes 4718592 | tf_op jit(solution)/shard_map/reduce_scatter | solution.py:195
  360.2 9.4 %copy-start.4 = (f32[16,128,16]{1,2,0:T(8,128)S(1)}, f32[16,128,16]{1,2,0:T(8,128)}, u32[]{:S(2)}) copy-start(f32[16,128,16]{1,2,0:T(8,128)} %custom-call.1) | copy-start | bytes 393220
  360.2 18.2 %copy-start.9 = (f32[16,128]{0,1:T(8,128)S(1)}, f32[16,128]{0,1:T(8,128)}, u32[]{:S(2)}) copy-start(f32[16,128]{0,1:T(8,128)} %copy-done.8) | copy-start | bytes 24580
  360.2 18.2 %copy-start.25 = (pred[16]{0:T(512)(128)(4,1)S(1)}, pred[16]{0:T(512)(128)(4,1)}, u32[]{:S(2)}) copy-start(pred[16]{0:T(512)(128)(4,1)} %get-tuple-element.507) | copy-start | bytes 52
  446.5 56.8 %copy-start.7 = (f32[16,128]{0,1:T(8,128)S(1)}, f32[16,128]{0,1:T(8,128)}, u32[]{:S(2)}) copy-start(f32[16,128]{0,1:T(8,128)} %copy-done.6) | copy-start | bytes 24580
  446.5 63.2 %copy-start.17 = (f32[2048]{0:T(1024)S(1)}, f32[2048]{0:T(1024)}, u32[]{:S(2)}) copy-start(f32[2048]{0:T(1024)} %param.21) | copy-start | bytes 24580
  498.7 19.1 %all-to-all-start = ((f32[4,16,2048]{2,1,0:T(8,128)}), f32[4,16,2048]{2,1,0:T(8,128)S(1)}, u32[]{:S(2)}, u32[]{:S(2)}) async-start(f32[4,16,2048]{2,1,0:T(8,128)} %reduce-scatter.2.cloned.1.call-done), calls=%async_computation.1 | async-start | bytes 1048576 | tf_op jit(solution)/shard_map/all_to_all | solution.py:196
  506.7 3.0 copy-start.5
  509.7 8.9 %copy-start.1 = (bf16[128,128]{1,0:T(8,128)(2,1)S(1)}, bf16[128,128]{1,0:T(8,128)(2,1)}, u32[]{:S(2)}) copy-start(bf16[128,128]{1,0:T(8,128)(2,1)} %param.18) | copy-start | bytes 98308
Sparse Core Ops, SparseCore 0:
  329.8 25.2 all-gather.3
  446.6 51.9 reduce-scatter.1
where the time goes:
time: 529 us; the launch traced here: 525 us
  local copies, waits for them, and re-layouts  306 us (58%)
  matrix products  68.6 us (13%)
  other arithmetic  57.8 us (11%)
  waiting for transfers between devices  56.3 us (11%)
  between operations  15 us (3%)
  blocking collectives  9.49 us (2%)
  starting transfers between devices  7.84 us (1%)
    gather x2, local copies, waits for them, and re-layouts, per_device(): tap_table = jnp.take(mr_filter, jnp.clip(tap_lag, 0, MR_LEN - 1), axis=0)  127 us
    gather x2, local copies, waits for them, and re-layouts, per_device(): jnp.take(li_taps, jnp.clip(tap_gap, 0, MR_LEN - 1), axis=1)  68.9 us
    reduce_scatter x1, waiting for transfers between devices, per_device(): lax.psum_scatter(slot_states, 'ctx', scatter_dimension=0, tiled=True)  52.1 us
    gather x2, local copies, waits for them, and re-layouts, per_device(): jnp.take(end_states, chosen, axis=0)  38.2 us
    dot_general x1, matrix products, per_device(): jnp.einsum('kngj,kjgc->kngc', end_weights, picked, precision=highest)  24.7 us
    dot_general x2, matrix products, li_block(): jnp.einsum('gij,jgc->igc', inner_kernel, values, precision=highest)  19.5 us
    gather x2, local copies, waits for them, and re-layouts, per_device(): jnp.take(mixed_blocks, block_pick, axis=0).astype(jnp.float32)  17.1 us
    dynamic_update_slice x8, local copies, waits for them, and re-layouts, per_device(): lax.scan(mr_block, jnp.zeros((), jnp.float32), (windows, starts_blocked,...  15.2 us
  transfers between devices with their start and end apart: 4, of which 2 were waited for; matrix products, arithmetic and copies ran while one was open for 53% of the time, Pallas kernels for 0%

commit v1 on v0

v1 whole, which is shorter than its diff:
```python
import functools

import jax
import jax.numpy as jnp
from jax import lax
from jax.experimental import pallas as pl
from jax.experimental.pallas import tpu as pltpu
from jax.sharding import PartitionSpec as P

TAPS = 128
ENDS = 16
LANES = 128
F32 = jnp.float32
BF16 = jnp.bfloat16

SMEM = pl.BlockSpec(memory_space=pltpu.SMEM)


def params(grid_dims):
    return pltpu.CompilerParams(
        dimension_semantics=("arbitrary",) * grid_dims, vmem_limit_bytes=48 * 1024 * 1024
    )


def iota(shape, dim):
    return lax.broadcasted_iota(jnp.int32, shape, dim)


def dot(a, b):
    return lax.dot_general(a, b, (((1,), (0,)), ((), ())), preferred_element_type=F32)


def dot_t(a, b):
    return lax.dot_general(a, b, (((0,), (0,)), ((), ())), preferred_element_type=F32)


def spread(x, first_group, size, lanes):
    groups = x.shape[1]
    pick = (iota((groups, lanes), 0) == first_group + iota((groups, lanes), 1) // size).astype(F32)
    pick = pick.astype(BF16)
    high = x.astype(BF16)
    rest = x - high.astype(F32)
    mid = rest.astype(BF16)
    low = (rest - mid.astype(F32)).astype(BF16)
    return dot(high, pick) + dot(mid, pick) + dot(low, pick)


def circulant(row):
    return pltpu.roll(
        jnp.broadcast_to(row, (TAPS, TAPS)), 0, 1, stride=1, stride_axis=0
    ).astype(BF16)


def states_kernel(
    cap,
    size,
    offsets,
    owners,
    place,
    halo,
    value,
    key,
    filt,
    rates,
    gains,
    resid,
    mixed_out,
    ends_out,
    spread_out,
    masks_out,
    taps_out,
    filter_rows,
    picks,
    flat,
    first_tok,
    last_tok,
):
    length = value.shape[0]
    poles, groups = rates.shape
    docs = offsets.shape[0] - 1
    peers = ends_out.shape[0]
    slots = owners.shape[0] // peers
    rows = peers * cap
    padded = picks.shape[0]
    tile = pl.program_id(0)
    per_tile = LANES // size
    begin = place[0] * length

    @pl.when(tile == 0)
    def prepare():
        spot = begin + iota((length, LANES), 0)

        def at(d, carry):
            off = offsets[d]
            return (
                jnp.where(spot >= off, off, carry[0]),
                jnp.where(off <= begin + length - 1, off, carry[1]),
            )

        starts, last_start = lax.fori_loop(
            0, docs, at, (jnp.zeros((length, LANES), jnp.int32), jnp.int32(0))
        )
        i, j = iota((TAPS, TAPS), 0), iota((TAPS, TAPS), 1)
        s0, s1 = starts[:TAPS], starts[TAPS:]
        cross = s1 <= begin + j
        for index, mask in enumerate(
            (
                (j > i) & (s0 <= begin - TAPS + j),
                (j <= i) & (s0 <= begin + j),
                (j > i) & cross,
                (j <= i) & (s1 <= begin + TAPS + j),
                (j <= i) & cross,
            )
        ):
            masks_out[index] = mask.astype(F32).astype(BF16)
        turn = (i == (TAPS - j) % TAPS).astype(F32).astype(BF16)
        filter_rows[...] = dot_t(filt[...], turn)
        lag = iota((TAPS, groups), 0).astype(F32)
        for half in range(2):
            total = jnp.zeros((TAPS, groups), F32)
            for n in range(poles):
                total = total + (resid[n : n + 1] * gains[n : n + 1]) * jnp.exp(
                    -rates[n : n + 1] * (lag + float(half * TAPS))
                )
            taps_out[half] = dot_t(total.astype(BF16), turn)

        first_tok[rows] = jnp.maximum(last_start - begin, 0)
        last_tok[rows] = length - 1
        for s in range(rows):
            r, parity = s // cap, s % cap

            def look(h, found, r=r, parity=parity):
                doc = owners[r * slots + h * cap + parity]
                end = offsets[doc + 1] - 1 - begin
                here = (end >= 0) & (end < length)
                return (
                    jnp.where(here, jnp.maximum(offsets[doc] - begin, 0), found[0]),
                    jnp.where(here, end, found[1]),
                )

            got = lax.fori_loop(0, slots // cap, look, (jnp.int32(1), jnp.int32(0)))
            first_tok[s] = got[0]
            last_tok[s] = got[1]
        row = iota((padded, length), 0)
        low = jnp.ones((padded, length), jnp.int32)
        high = jnp.zeros((padded, length), jnp.int32)
        for s in range(rows + 1):
            low = jnp.where(row == s, first_tok[s], low)
            high = jnp.where(row == s, last_tok[s], high)
        token = iota((padded, length), 1)
        picks[...] = ((token >= low) & (token <= high)).astype(F32).astype(BF16)

    group_rows = filter_rows[pl.ds(tile * per_tile, per_tile), :]
    window0 = jnp.concatenate([halo[...], value[:TAPS]], axis=0)
    window1 = value[...]
    lane_group = iota((TAPS, LANES), 1) // size
    acc0 = jnp.zeros((TAPS, LANES), F32)
    acc1 = jnp.zeros((TAPS, LANES), F32)
    for g in range(per_tile):
        c = circulant(group_rows[g : g + 1])
        y0 = dot(jnp.concatenate([c * masks_out[0], c * masks_out[1]], axis=1), window0)
        y1 = dot(jnp.concatenate([c * masks_out[2], c * masks_out[3]], axis=1), window1)
        acc0 = jnp.where(lane_group == g, y0, acc0)
        acc1 = jnp.where(lane_group == g, y1, acc1)
    mixed = (key[...].astype(F32) * jnp.concatenate([acc0, acc1], axis=0)).astype(BF16)
    mixed_out[...] = mixed
    wide = mixed.astype(F32)

    p = spread(rates[...], tile * per_tile, size, LANES)
    beta = spread(gains[...], tile * per_tile, size, LANES)
    spread_out[...] = p
    step = 16
    near = iota((step, LANES), 0).astype(F32)
    for n in range(poles):
        pn = p[n : n + 1]
        grow = jnp.exp(pn * near)
        jump = jnp.broadcast_to(jnp.exp(pn * float(step)), (step, LANES))
        parts = []
        for k in range(length // step):
            parts.append((grow * wide[k * step : (k + 1) * step]).astype(BF16))
            grow = grow * jump
        flat[n * padded : (n + 1) * padded, :] = dot(picks[...], jnp.concatenate(parts, axis=0))
    for s in range(rows + 1):
        state = flat[pl.ds(s, poles, stride=padded), :]
        state = state * jnp.exp(-p * last_tok[s].astype(F32)) * beta
        state = state.astype(BF16)
        if s < rows:
            ends_out[s // cap, s % cap] = state
        else:
            for r in range(peers):
                ends_out[r, cap] = state


def local_kernel(size, mixed, masks, taps, skip, local_out):
    tile = pl.program_id(0)
    per_tile = LANES // size
    rows_a = taps[0, pl.ds(tile * per_tile, per_tile), :]
    rows_b = taps[1, pl.ds(tile * per_tile, per_tile), :]
    lane_group = iota((TAPS, LANES), 1) // size
    acc0 = jnp.zeros((TAPS, LANES), F32)
    acc1 = jnp.zeros((TAPS, LANES), F32)
    x = mixed[...]
    for g in range(per_tile):
        a, b = circulant(rows_a[g : g + 1]), circulant(rows_b[g : g + 1])
        y0 = dot(a * masks[1], x[:TAPS])
        y1 = dot(jnp.concatenate([a * masks[2] + b * masks[4], a * masks[3]], axis=1), x)
        acc0 = jnp.where(lane_group == g, y0, acc0)
        acc1 = jnp.where(lane_group == g, y1, acc1)
    local_out[...] = jnp.concatenate([acc0, acc1], axis=0) + skip[...] * x.astype(F32)


def slots_kernel(length, offsets, owners, place, got, rates, slot_out, entering_out):
    peers, cap = got.shape[0], got.shape[1] - 1
    slots = slot_out.shape[0]
    docs = offsets.shape[0] - 1
    me = place[0]
    p = rates[...]
    fade = jnp.exp(-p * float(length))

    def entering(first, stop):
        def hop(c, state):
            return fade * state + got[c, cap].astype(F32)

        return lax.fori_loop(first, stop, hop, jnp.zeros(p.shape, F32))

    def at(d, start):
        return jnp.where(offsets[d] <= me * length, offsets[d], start)

    my_start = lax.fori_loop(0, docs, at, jnp.int32(0))
    entering_out[...] = entering(my_start // length, me)
    for k in range(slots):
        doc = owners[me * slots + k]
        start, end = offsets[doc], offsets[doc + 1] - 1
        source = end // length
        gain = jnp.exp(-p * (end - source * length + 1).astype(F32))
        state = got[source, k % cap].astype(F32) + gain * entering(start // length, source)
        slot_out[k] = state.astype(BF16)


def output_kernel(length, size, offsets, place, query, local, entering, rates, resid, out):
    docs = offsets.shape[0] - 1
    begin = place[0] * length
    poles, width = entering.shape

    def at(d, limit):
        return jnp.where(
            (offsets[d] < begin) & (offsets[d + 1] > begin), offsets[d + 1] - begin, limit
        )

    limit = lax.fori_loop(0, docs, at, jnp.int32(0))
    t = iota((length, width), 0)
    weight = jnp.exp(-rates[...] * (t + 1).astype(F32)) * resid[...]
    weight = jnp.where(t < limit, weight, 0.0)
    w_high = weight.astype(BF16)
    w_low = (weight - w_high.astype(F32)).astype(BF16)
    e = entering[...]
    e_high = e.astype(BF16)
    e_low = (e - e_high.astype(F32)).astype(BF16)
    kept = iota((width, width), 0) // poles == iota((width, width), 1) // size
    kept = kept.astype(F32).astype(BF16)
    b_high = jnp.concatenate([e_high] * (width // size), axis=0) * kept
    b_low = jnp.concatenate([e_low] * (width // size), axis=0) * kept
    fix = dot(w_high, b_high) + dot(w_low, b_high) + dot(w_high, b_low)
    out[...] = (query[...].astype(F32) * (local[...] + fix)).astype(BF16)


def widen_kernel(x, out):
    out[...] = x[...].astype(F32)


def per_device(query, key, value, filt, rates, resid, skip, offsets, owners):
    length, width = value.shape
    poles, groups = rates.shape
    size = width // groups
    peers, lines = lax.axis_size("ctx"), lax.axis_size("ch")
    slots = owners.shape[0] // peers
    cap = -(-ENDS // peers)
    rows = peers * cap
    padded = -(-(rows + 1) // 16) * 16
    place = lax.axis_index("ctx").astype(jnp.int32).reshape(1)
    gains = jnp.sqrt(-jnp.expm1(-2.0 * rates))
    rates_flat = rates.T.reshape(1, groups * poles)
    resid_flat = resid.T.reshape(1, groups * poles)

    halo = lax.ppermute(
        value[length - TAPS :], "ctx", [(i, i + 1) for i in range(peers - 1)]
    )

    def whole(shape):
        return pl.BlockSpec(shape, lambda i: (0,) * len(shape))

    def lanes(height, w=LANES):
        return pl.BlockSpec((height, w), lambda i: (0, i))

    mixed, ends, rates_wide, masks, taps = pl.pallas_call(
        functools.partial(states_kernel, cap, size),
        grid=(width // LANES,),
        in_specs=[
            SMEM,
            SMEM,
            SMEM,
            lanes(TAPS),
            lanes(length),
            lanes(length),
            whole((TAPS, groups)),
            whole((poles, groups)),
            whole((poles, groups)),
            whole((poles, groups)),
        ],
        out_specs=[
            lanes(length),
            pl.BlockSpec((peers, cap + 1, poles, LANES), lambda i: (0, 0, 0, i)),
            lanes(poles),
            whole((5, TAPS, TAPS)),
            whole((2, groups, TAPS)),
        ],
        out_shape=[
            jax.ShapeDtypeStruct((length, width), BF16),
            jax.ShapeDtypeStruct((peers, cap + 1, poles, width), BF16),
            jax.ShapeDtypeStruct((poles, width), F32),
            jax.ShapeDtypeStruct((5, TAPS, TAPS), BF16),
            jax.ShapeDtypeStruct((2, groups, TAPS), F32),
        ],
        scratch_shapes=[
            pltpu.VMEM((groups, TAPS), F32),
            pltpu.VMEM((padded, length), BF16),
            pltpu.VMEM((poles * padded, LANES), F32),
            pltpu.SMEM((padded,), jnp.int32),
            pltpu.SMEM((padded,), jnp.int32),
        ],
        compiler_params=params(1),
        name="states",
    )(offsets, owners, place, halo, value, key, filt, rates, gains, resid)

    got = lax.all_to_all(ends, "ctx", split_axis=0, concat_axis=0, tiled=True)

    local = pl.pallas_call(
        functools.partial(local_kernel, size),
        grid=(width // LANES,),
        in_specs=[
            lanes(length),
            whole((5, TAPS, TAPS)),
            whole((2, groups, TAPS)),
            lanes(1),
        ],
        out_specs=lanes(length),
        out_shape=jax.ShapeDtypeStruct((length, width), F32),
        compiler_params=params(1),
        cost_estimate=pl.CostEstimate(
            flops=2 * 2 * length * length * width * 8, bytes_accessed=6 * length * width, transcendentals=0
        ),
        name="local",
    )(mixed, masks, taps, skip.reshape(1, width))

    picked, entering = pl.pallas_call(
        functools.partial(slots_kernel, length),
        in_specs=[SMEM, SMEM, SMEM] + [pl.BlockSpec(memory_space=pltpu.VMEM)] * 2,
        out_specs=[pl.BlockSpec(memory_space=pltpu.VMEM)] * 2,
        out_shape=[
            jax.ShapeDtypeStruct((slots, poles, width), BF16),
            jax.ShapeDtypeStruct((poles, width), F32),
        ],
        compiler_params=params(0),
        name="slots",
    )(offsets, owners, place, got, rates_wide)

    gathered = lax.all_to_all(picked, "ch", split_axis=0, concat_axis=0, tiled=True)

    tile = 2 * LANES
    output = pl.pallas_call(
        functools.partial(output_kernel, length, size),
        grid=(width // tile,),
        in_specs=[
            SMEM,
            SMEM,
            lanes(length, tile),
            lanes(length, tile),
            lanes(poles, tile),
            lanes(1, tile),
            lanes(1, tile),
        ],
        out_specs=lanes(length, tile),
        out_shape=jax.ShapeDtypeStruct((length, width), BF16),
        compiler_params=params(1),
        cost_estimate=pl.CostEstimate(
            flops=6 * length * tile * width, bytes_accessed=8 * length * width, transcendentals=0
        ),
        name="output",
    )(offsets, place, query, local, entering, rates_flat, resid_flat)

    per_line = slots // lines
    doc_states = pl.pallas_call(
        widen_kernel,
        grid=(lines,),
        in_specs=[pl.BlockSpec((per_line, poles, width), lambda h: (h, 0, 0))],
        out_specs=pl.BlockSpec((per_line, poles, width), lambda h: (0, 0, h)),
        out_shape=jax.ShapeDtypeStruct((per_line, poles, lines * width), F32),
        compiler_params=params(1),
        name="widen",
    )(gathered)
    return (output, doc_states)


def solution(mesh):
    placed = (
        P("ctx", "ch"),
        P("ctx", "ch"),
        P("ctx", "ch"),
        P(None, "ch"),
        P(None, "ch"),
        P(None, "ch"),
        P("ch"),
        P(),
        P(),
    )
    return jax.shard_map(
        per_device,
        mesh=mesh,
        in_specs=placed,
        out_specs=(P("ctx", "ch"), P(("ctx", "ch"), None, None)),
        check_vma=False,
    )
```

time: 529 us -> 88.1 us (0.17)
  local copies, waits for them, and re-layouts: 306 us -> 6.26 us
  matrix products: 68.6 us -> 0 us
  other arithmetic: 57.8 us -> 0.71 us
  Pallas kernels: 0 us -> 39.3 us
  waiting for transfers between devices: 56.3 us -> 21.4 us
  between operations: 15 us -> 0.72 us
  starting transfers between devices: 7.84 us -> 19.2 us
  blocking collectives: 9.49 us -> 0 us
    gather x9 -> x0, local copies, waits for them, and re-layouts: 260 us -> none  [the longest x2 127 us: per_device(): tap_table = jnp.take(mr_filter, jnp.clip(tap_lag, 0, MR_LEN - 1), axis=0)]
    dot_general x10 -> x0, matrix products: 68.6 us -> none  [the longest x1 24.7 us: per_device(): jnp.einsum('kngj,kjgc->kngc', end_weights, picked, precision=highest)]
    reduce_scatter x1 -> x0, waiting for transfers between devices: 52.1 us -> none  [per_device(): lax.psum_scatter(slot_states, 'ctx', scatter_dimension=0, tiled=True)]
    pallas_call x0 -> x5, Pallas kernels: none -> 39.3 us  [the longest x1 20.1 us: per_device(): pl.pallas_call(functools.partial(states_kernel, cap, size), grid=(width /...]
    select_n x13 -> x0, other arithmetic: 29.4 us -> none  [the longest x1 8.62 us: per_device(): jnp.where((tap_gap >= 0)[None], jnp.take(li_taps, jnp.clip(tap_gap, 0, MR...]
    all_to_all x1 -> x2, waiting for transfers between devices: 4.19 us -> 20.6 us  [the longest x1 20.6 us: per_device(): got = lax.all_to_all(ends, 'ctx', split_axis=0, concat_axis=0, tiled=True)]
    dynamic_update_slice x8 -> x0, local copies, waits for them, and re-layouts: 15.2 us -> none  [per_device(): lax.scan(mr_block, jnp.zeros((), jnp.float32), (windows, starts_blocked,...]
    all_to_all x1 -> x2, starting transfers between devices: 4.62 us -> 16.8 us  [the longest x1 11.9 us: per_device(): got = lax.all_to_all(ends, 'ctx', split_axis=0, concat_axis=0, tiled=True)]
  transfers between devices with their start and end apart: 4 -> 3, of which waited for: 2 -> 2; matrix products, arithmetic and copies ran while one was open for 53% -> 1% of each run, Pallas kernels for 0% -> 18%
where the time goes in v1:
time: 88.1 us; the launch traced here: 87.5 us
  Pallas kernels  39.3 us (45%)
  waiting for transfers between devices  21.4 us (24%)
  starting transfers between devices  19.2 us (22%)
  local copies, waits for them, and re-layouts  6.26 us (7%)
    all_to_all x1, waiting for transfers between devices, per_device(): got = lax.all_to_all(ends, 'ctx', split_axis=0, concat_axis=0, tiled=True)  20.6 us
    pallas_call x1, Pallas kernels, per_device(): pl.pallas_call(functools.partial(states_kernel, cap, size), grid=(width /...  20.1 us
    all_to_all x1, starting transfers between devices, per_device(): got = lax.all_to_all(ends, 'ctx', split_axis=0, concat_axis=0, tiled=True)  11.9 us
    pallas_call x1, Pallas kernels, per_device(): pl.pallas_call(functools.partial(output_kernel, length, size), grid=(widt...  8.59 us
    pallas_call x1, Pallas kernels, per_device(): pl.pallas_call(functools.partial(local_kernel, size), grid=(width // LANE...  7.34 us
    all_to_all x1, starting transfers between devices, per_device(): lax.all_to_all(picked, 'ch', split_axis=0, concat_axis=0, tiled=True)  4.87 us
    unnamed x26, local copies, waits for them, and re-layouts  4.71 us
    ppermute x1, starting transfers between devices, per_device(): lax.ppermute(value[length - TAPS:], 'ctx', [(i, i + 1) for i in range(pee...  2.39 us
  transfers between devices with their start and end apart: 3, of which 2 were waited for; matrix products, arithmetic and copies ran while one was open for 1% of the time, Pallas kernels for 18%

profile of v1, /device:TPU:0, one launch (start us, length us, event | category | flops | bytes accessed | tf_op | source)
XLA Modules:
  0.0 87.5 jit_solution(18264228553789404127)
XLA Ops:
  0.6 0.0 copy-start
  0.6 1.2 %slice.3 = bf16[128,2048]{1,0:T(8,128)(2,1)S(1)} slice(bf16[256,2048]{1,0:T(8,128)(2,1)} %value.1), slice={[128:256], [0:2048]} | slice | bytes 1048576 | tf_op jit(solution)/shard_map/slice | solution.py:286
  1.8 2.4 %collective-permute-start = (bf16[128,2048]{1,0:T(8,128)(2,1)S(1)}, bf16[128,2048]{1,0:T(8,128)(2,1)S(1)}, u32[]{:S(2)}, u32[]{:S(2)}) collective-permute-start(bf16[128,2048]{1,0:T(8,128)(2,1)S(1)} %slice.3), channel_id=1, source_target_pairs={{0,4},{4,8},{8,12},{12,16},{16,20},{20,24},{24,28},{1,5},{5,9},{9,... | collective-permute-start | bytes 1572872 | tf_op jit(solution)/shard_map/ppermute | solution.py:285
  4.2 0.7 negate_sqrt_fusion.gains
  4.9 0.8 collective-permute-done.halo
  5.7 0.0 copy-done
  5.7 0.0 copy-start.2
  5.7 1.2 %copy-done.2 = bf16[256,2048]{1,0:T(8,128)(2,1)S(1)} copy-done((bf16[256,2048]{1,0:T(8,128)(2,1)S(1)}, bf16[256,2048]{1,0:T(8,128)(2,1)}, u32[]{:S(2)}) %copy-start.2) | copy-done | bytes 1048600
  6.9 0.0 copy-start.3
  6.9 0.7 copy-done.3
  7.6 0.0 copy-start.5
  7.6 0.8 copy-done.5
  8.4 0.0 copy-start.6
  8.4 0.7 copy-done.6
  9.1 0.0 copy-start.8
  9.1 0.7 copy-done.8
  9.7 0.0 copy-start.10
  9.7 0.7 copy-done.10
  10.4 20.1 %states.1 = (bf16[256,2048]{1,0:T(8,128)(2,1)S(1)}, bf16[8,3,16,2048]{3,2,1,0:T(8,128)(2,1)}, f32[16,2048]{1,0:T(8,128)S(1)}, bf16[5,128,128]{2,1,0:T(8,128)(2,1)S(1)}, f32[2,128,128]{2,1,0:T(8,128)S(1)}) custom-call(s32[65]{0:T(128)S(1)} %copy-done.8, s32[32]{0:T(128)S(1)} %copy-done.10, s32[1]{0:T(128)} %bitcast.place, ...), custom_call_target="tpu_custom_call" | custom-call | tf_op jit(solution)/shard_map/states/pallas_call | solution.py:295
  30.5 0.0 copy-start.4
  30.5 0.0 copy-start.7
  30.5 0.0 copy-start.9
  30.5 0.0 copy-start.11
  30.5 11.9 %all-to-all-start = ((bf16[8,3,16,2048]{3,2,1,0:T(8,128)(2,1)}), bf16[8,3,16,2048]{3,2,1,0:T(8,128)(2,1)S(1)}, u32[]{:S(2)}, u32[]{:S(2)}) async-start(bf16[8,3,16,2048]{3,2,1,0:T(8,128)(2,1)} %get-tuple-element.12), calls=%async_computation | async-start | bytes 3145728 | tf_op jit(solution)/shard_map/all_to_all | solution.py:335
  42.4 0.0 copy-start.12
  42.4 0.0 copy-done.4
  42.5 0.1 copy.13
  42.6 0.1 reshape.18.rates
  42.7 0.0 copy-done.7
  42.7 0.1 copy.14
  42.8 0.1 reshape.19.resid
  42.9 20.6 %all-to-all-done.got = bf16[8,3,16,2048]{3,2,1,0:T(8,128)(2,1)S(1)} async-done(((bf16[8,3,16,2048]{3,2,1,0:T(8,128)(2,1)}), bf16[8,3,16,2048]{3,2,1,0:T(8,128)(2,1)S(1)}, u32[]{:S(2)}, u32[]{:S(2)}) %all-to-all-start) | async-done | bytes 1572896 | tf_op jit(solution)/shard_map/all_to_all | solution.py:335
  63.5 0.0 copy-done.9
  63.5 0.0 copy-done.11
  63.5 1.8 %slots.1 = (bf16[4,16,2048]{2,1,0:T(8,128)(2,1)}, f32[16,2048]{1,0:T(8,128)S(1)}) custom-call(s32[65]{0:T(128)S(1)} %copy-done.9, s32[32]{0:T(128)S(1)} %copy-done.11, s32[1]{0:T(128)} %bitcast.place, bf16[8,3,16,2048]{3,2,1,0:T(8,128)(2,1)S(1)} %all-to-all-done.got, f32[16,2048]{1,0:T(8,128)S(1)} %get-tuple-element.13.rates), custom_call_target="tpu_custom_call" | custom-call | tf_op jit(solution)/shard_map/slots/pallas_call | solution.py:355
  65.3 4.9 %all-to-all-start.1 = ((bf16[4,16,2048]{2,1,0:T(8,128)(2,1)}), bf16[4,16,2048]{2,1,0:T(8,128)(2,1)S(1)}, u32[]{:S(2)}, u32[]{:S(2)}) async-start(bf16[4,16,2048]{2,1,0:T(8,128)(2,1)} %get-tuple-element.15), calls=%async_computation.1 | async-start | bytes 524288 | tf_op jit(solution)/shard_map/all_to_all | solution.py:367
  70.2 0.0 copy-done.12
  70.2 0.0 copy-start.1
  70.2 7.3 %local.1 = f32[256,2048]{1,0:T(8,128)S(1)} custom-call(bf16[256,2048]{1,0:T(8,128)(2,1)S(1)} %get-tuple-element.9.mixed, bf16[5,128,128]{2,1,0:T(8,128)(2,1)S(1)} %get-tuple-element.10.masks, f32[2,128,128]{2,1,0:T(8,128)S(1)} %get-tuple-element.11.taps, f32[1,2048]{1,0:T(1,128)S(1)} %bitcast.6), custom_call_target="tpu_custom_call" | custom-call | flops 4294967296 | bytes 3145728 | tf_op jit(solution)/shard_map/local/pallas_call | solution.py:337
  77.5 0.0 copy-done.1
  77.5 8.6 %output.1 = bf16[256,2048]{1,0:T(8,128)(2,1)} custom-call(s32[65]{0:T(128)S(1)} %copy-done.9, s32[1]{0:T(128)} %bitcast.place, bf16[256,2048]{1,0:T(8,128)(2,1)S(1)} %copy-done.1, f32[256,2048]{1,0:T(8,128)S(1)} %local.1, f32[16,2048]{1,0:T(8,128)S(1)} %get-tuple-element.14.entering, f32[1,2048]{1,0:T(1,128)S(1)} %reshape.18.rates, f32[1,2048]{1,0:T(1,128)S(1)} %reshape.19.resid), custom_call_target="tpu_custom_call" | custom-call | flops 805306368 | bytes 4194304 | tf_op jit(solution)/shard_map/output/pallas_call | solution.py:370
  86.1 0.0 all-to-all-done.1.x
  86.1 1.4 %widen.1 = f32[1,16,8192]{2,1,0:T(8,128)} custom-call(bf16[4,16,2048]{2,1,0:T(8,128)(2,1)S(1)} %all-to-all-done.1.x), custom_call_target="tpu_custom_call" | custom-call | tf_op jit(solution)/shard_map/widen/pallas_call | solution.py:392
Async XLA Ops:
  0.6 5.1 %copy-start = (bf16[256,2048]{1,0:T(8,128)(2,1)S(1)}, bf16[256,2048]{1,0:T(8,128)(2,1)}, u32[]{:S(2)}) copy-start(bf16[256,2048]{1,0:T(8,128)(2,1)} %value.1) | copy-start | bytes 3145732
  1.8 3.9 %collective-permute-start = (bf16[128,2048]{1,0:T(8,128)(2,1)S(1)}, bf16[128,2048]{1,0:T(8,128)(2,1)S(1)}, u32[]{:S(2)}, u32[]{:S(2)}) collective-permute-start(bf16[128,2048]{1,0:T(8,128)(2,1)S(1)} %slice.3), channel_id=1, source_target_pairs={{0,4},{4,8},{8,12},{12,16},{16,20},{20,24},{24,28},{1,5},{5,9},{9,... | collective-permute-start | bytes 1572872 | tf_op jit(solution)/shard_map/ppermute | solution.py:285
  5.7 1.2 %copy-start.2 = (bf16[256,2048]{1,0:T(8,128)(2,1)S(1)}, bf16[256,2048]{1,0:T(8,128)(2,1)}, u32[]{:S(2)}) copy-start(bf16[256,2048]{1,0:T(8,128)(2,1)} %key.1) | copy-start | bytes 3145732
  6.9 0.7 copy-start.3
  7.6 0.8 copy-start.5
  8.4 0.7 copy-start.6
  9.1 0.7 copy-start.8
  9.7 0.7 copy-start.10
  30.5 12.0 %copy-start.4 = (f32[16,128]{1,0:T(8,128)S(1)}, f32[16,128]{1,0:T(8,128)}, u32[]{:S(2)}) copy-start(f32[16,128]{1,0:T(8,128)} %rates.1) | copy-start | bytes 24580
  30.5 12.2 %copy-start.7 = (f32[16,128]{1,0:T(8,128)S(1)}, f32[16,128]{1,0:T(8,128)}, u32[]{:S(2)}) copy-start(f32[16,128]{1,0:T(8,128)} %resid.1) | copy-start | bytes 24580
  30.5 33.0 %copy-start.9 = (s32[65]{0:T(128)S(1)}, s32[65]{0:T(128)}, u32[]{:S(2)}) copy-start(s32[65]{0:T(128)} %offsets.5) | copy-start | bytes 784
  30.5 33.0 %copy-start.11 = (s32[32]{0:T(128)S(1)}, s32[32]{0:T(128)}, u32[]{:S(2)}) copy-start(s32[32]{0:T(128)} %owners.3) | copy-start | bytes 388
  30.5 33.0 %all-to-all-start = ((bf16[8,3,16,2048]{3,2,1,0:T(8,128)(2,1)}), bf16[8,3,16,2048]{3,2,1,0:T(8,128)(2,1)S(1)}, u32[]{:S(2)}, u32[]{:S(2)}) async-start(bf16[8,3,16,2048]{3,2,1,0:T(8,128)(2,1)} %get-tuple-element.12), calls=%async_computation | async-start | bytes 3145728 | tf_op jit(solution)/shard_map/all_to_all | solution.py:335
  42.4 27.7 %copy-start.12 = (f32[2048]{0:T(1024)S(1)}, f32[2048]{0:T(1024)}, u32[]{:S(2)}) copy-start(f32[2048]{0:T(1024)} %param.15) | copy-start | bytes 24580
  65.3 20.8 %all-to-all-start.1 = ((bf16[4,16,2048]{2,1,0:T(8,128)(2,1)}), bf16[4,16,2048]{2,1,0:T(8,128)(2,1)S(1)}, u32[]{:S(2)}, u32[]{:S(2)}) async-start(bf16[4,16,2048]{2,1,0:T(8,128)(2,1)} %get-tuple-element.15), calls=%async_computation.1 | async-start | bytes 524288 | tf_op jit(solution)/shard_map/all_to_all | solution.py:367
  70.2 7.3 %copy-start.1 = (bf16[256,2048]{1,0:T(8,128)(2,1)S(1)}, bf16[256,2048]{1,0:T(8,128)(2,1)}, u32[]{:S(2)}) copy-start(bf16[256,2048]{1,0:T(8,128)(2,1)} %query.1) | copy-start | bytes 3145732
